TPU v7x, 256 devices: a whole 4x4x8 slice. The times are simulated.
256 devices in a mesh: space: 128 (over x, z, y), chan: 2 (over core).
Axes of the slice: x: 4, y: 4, z: 8, core: 2. Of those that a mesh axis runs over, the one named last changes fastest.
Arguments:
- features: bfloat16 [1024, 512, 128], P('space', None, 'chan'), may hold values from -6 to 6
- heights: int32 [1024, 64], P('space'), may hold values from 0 to 8
- neighbours: int32 [128, 26], P('space'), may hold values from -1 to 127, as said below
- w_conv: bfloat16 [27, 128, 128], replicated, may hold values from -0.109375 to 0.109375
- w_down: bfloat16 [8, 128, 256], replicated, may hold values from -0.1875 to 0.1875
- cotangent: bfloat16 [128, 512, 256], P('space'), may hold values from -12 to 12
Outputs:
- coarse: bfloat16 [128, 512, 256], P('space', None, 'chan')
- grad_conv: float32 [27, 128, 128], P(None, 'chan')
- grad_down: float32 [8, 128, 256], P(None, None, 'chan')
- grad_features: bfloat16 [1024, 512, 128], P('space', None, 'chan')
Inputs may be any that keep to these rules, and one draw needn't show every extreme that they name: neighbours[s, k] is the block at offset d_k from block s (the 26 offsets of the finite set (-1,0,1)^3 without the anchor, lexicographic in (x, y, z)), or -1 where no block is there; if neighbours[s, k] = q then neighbours[q, 25 - k] = s; distinct offsets name distinct blocks; blocks lie on a strip two positions wide and two high and are numbered in order of x, then y, then z, so that every neighbour q of s has 1 <= |q - s| <= 7.
All inputs are finite; a program needn't handle non-finite values.
Results may differ from a plain program's by a relative error of at most 0.005.
Values may be sent and summed in bfloat16 or wider, within the bound.
A program may use at most 320 MiB of HBM per device.

v0:
```python
import jax
import jax.numpy as jnp
from jax import lax
from jax.experimental import pallas as pl
from jax.experimental.pallas import tpu as pltpu
from jax.sharding import PartitionSpec as P

MESH = pl.DeviceIdType.MESH
F32 = jnp.float32
BF16 = jnp.bfloat16
MID = slice(128, 256)
XS, ZS, YS = 4, 8, 4
BLOCKS = XS * ZS * YS


def dot(a, b):
    return jnp.dot(a, b, preferred_element_type=F32)


def dot_t(a, b):
    return lax.dot_general(a, b, (((1,), (1,)), ((), ())), preferred_element_type=F32)


def kernel(
    heights, near, feat, w_conv, w_down, cot,
    coarse, g_conv, g_down, g_feat,
    pad, gpad, mask, up, vol, cat, hid, patches, turned, w_back, out_bricks,
    shift_a, shift_b, margin,
    faces, edges, y_low_0, y_low_1, y_high_0, y_high_1, z_low, z_high, far_0, far_1, far_edge_0, far_edge_1,
    coarse_st, down_st, down_in, conv_st, conv_in,
    c_bf, c_in, c_mid, c_in2, c_tot, c_all,
    d_bf, d_in, d_mid, d_in2, d_tot, d_mix, d_all,
    halo_s, halo_r, pair_s, pair_r,
    c1_s, c1_r, c2_s, c2_r, c3_s, c3_r, c4_s, c4_r,
    d1_s, d1_r, d2_s, d2_r, d3_s, d3_r, d4_s, d4_r,
):
    y_low, y_high = (y_low_0, y_low_1), (y_high_0, y_high_1)
    far, far_edge = (far_0, far_1), (far_edge_0, far_edge_1)
    s = lax.axis_index("space")
    m = lax.axis_index("chan")
    other = 1 - m
    sign = 2 * m - 1
    my_y = s % YS
    my_z = s // YS % ZS
    my_x = s // (YS * ZS)
    plane = my_x * YS + my_y
    wrap = lambda index: (index + 2 * BLOCKS) % BLOCKS
    plane_steps = [(a, b) for a in range(XS) for b in range(YS) if (a, b) != (0, 0)]

    def plane_peer(step):
        x, y = (my_x + step[0]) % XS, (my_y + step[1]) % YS
        return x * YS + y, ((x * ZS + my_z) * YS + y, m)

    def line_peer(step):
        z = (my_z + step) % ZS
        return z, ((my_x * ZS + z) * YS + my_y, m)

    def remote(src, dst, send, recv, device):
        return pltpu.make_async_remote_copy(
            src_ref=src, dst_ref=dst, send_sem=send, recv_sem=recv, device_id=device, device_id_type=MESH
        )

    barrier = pltpu.get_barrier_semaphore()
    greeted = [(s, other)]
    for d in (1, 2, 3):
        for e in (d, -d):
            greeted += [(wrap(s + e), m), (wrap(s + e), other)]
    greeted += [(wrap(s + sign * j), other) for j in (4, 5, 6, 7)]
    greeted += [plane_peer(step)[1] for step in plane_steps]
    greeted += [line_peer(step)[1] for step in range(1, ZS)]
    for device in greeted:
        pl.semaphore_signal(barrier, inc=1, device_id=device, device_id_type=MESH)

    levels = lax.broadcasted_iota(jnp.int32, (8, 128), 0)

    def mask_plane(x, _):
        for y in range(16):
            for z in range(2):
                height = heights[m + 2 * (y // 8) + 4 * z, x * 8 + y % 8]
                mask[x, y, 8 * z:8 * z + 8, :] = jnp.where(levels < height, 1.0, 0.0)
        return 0

    lax.fori_loop(0, 8, mask_plane, 0)
    own_cot = cot[pl.ds(pl.multiple_of(m * 256, 256), 256), :]

    def upstream(t, _):
        rows = w_down[pl.ds(pl.multiple_of(t * 256, 256), 256), :]
        got = dot_t(own_cot, rows)
        for z in range(2):
            part = got[:, 128 * z:128 * z + 128].reshape(4, 8, 8, 128)
            for x in range(4):
                up[x, t // 2, :, t % 2, pl.ds(z, 8, stride=2), :] = part[x]
        return 0

    lax.fori_loop(0, 4, upstream, 0)

    def turn_back(tap, _):
        w_back[tap] = w_conv[26 - tap].astype(F32).T.astype(BF16)
        return 0

    lax.fori_loop(0, 27, turn_back, 0)

    pl.semaphore_wait(barrier, len(greeted))

    pair = (s, other)
    own_rows = pl.ds(pl.multiple_of(m * 64, 64), 64)
    other_rows = pl.ds(pl.multiple_of(other * 64, 64), 64)
    swap = remote(feat.at[:, other], cat.at[:, own_rows, :], pair_s.at[0], pair_r.at[0], pair)
    swap.start()
    cat[:, own_rows, :] = feat[:, m]
    swap.wait()

    for oy in range(2):
        for half in range(2):
            columns = slice(256 * half, 256 * half + 256)
            low = cat[oy, :, columns].astype(F32).T.reshape(4, 8, 8, 128)
            high = cat[oy + 2, :, columns].astype(F32).T.reshape(4, 8, 8, 128)
            both = jnp.concatenate([low, high], axis=2)
            at = slice(4 * half, 4 * half + 4)
            both = both * mask[at, 8 * oy:8 * oy + 8]
            vol[at, 8 * oy:8 * oy + 8] = both
            pad[1 + 4 * half:5 + 4 * half, 1 + 8 * oy:9 + 8 * oy, :, MID] = both.astype(BF16)

    near_own = 8 - 7 * m
    far_own = 1 + 7 * m
    near_margin_there = 9 * m
    far_margin = 9 * m

    def halo_copies(space, turn):
        copies = []

        def add(src, dst, device):
            at = len(copies)
            copies.append(remote(src, dst, halo_s.at[turn, at], halo_r.at[turn, at], device))

        add(space.at[near_own, 1:17, :, MID], space.at[near_margin_there, 1:17, :, MID], pair)
        for j in range(1, 8):
            there = (wrap(s + sign * j), other)
            if j <= 4:
                add(space.at[far_own, 1:17, :, MID], far[turn].at[j - 1], there)
            add(edges.at[turn], far_edge[turn].at[j - 1], there)
        for j in range(1, 4):
            for step, row, landing in ((j, 16, y_low[turn]), (-j, 1, y_high[turn])):
                at = wrap(s + step)
                add(space.at[1:9, row, :, MID], landing.at[j - 1, 1:9], (at, m))
                add(space.at[near_own, row, :, MID], landing.at[j - 1, near_margin_there], (at, other))
        for step, face, landing in ((1, 1, z_low), (-1, 0, z_high)):
            at = wrap(s + step)
            add(faces.at[turn, face], landing.at[turn, 1:9], (at, m))
            add(faces.at[turn, face, near_own - 1], landing.at[turn, near_margin_there], (at, other))
        return copies

    def stage(space, turn):
        def one(x, _):
            for face, z in ((0, 0), (1, 15)):
                got = vol.at[x].reshape(256, 128)[pl.ds(z, 16, stride=16), :]
                faces[turn, face, x] = got.astype(BF16)
            return 0

        lax.fori_loop(0, 8, one, 0)
        edges[turn, 0] = faces[turn, 0, far_own - 1]
        edges[turn, 1] = space[far_own, 1, :, MID]
        edges[turn, 2] = space[far_own, 16, :, MID]
        edges[turn, 3] = faces[turn, 1, far_own - 1]

    zero = jnp.zeros((), BF16)

    def fill(space, turn):
        def beside(k):
            got = near[0, k]
            return got >= 0, got - s

        there, d = beside(15)
        space[:, 17, :, MID] = jnp.where(there, y_high[turn][jnp.clip(d - 1, 0, 2)], zero)
        there, d = beside(10)
        space[:, 0, :, MID] = jnp.where(there, y_low[turn][jnp.clip(-d - 1, 0, 2)], zero)
        there, d = beside(13)
        margin[1, :, 1:17, :] = jnp.where(there, z_high[turn], zero).astype(F32)
        there, d = beside(12)
        margin[0, :, 1:17, :] = jnp.where(there, z_low[turn], zero).astype(F32)
        for k, landing, to, z in ((16, y_high, 17, 1), (14, y_high, 17, 0), (11, y_low, 0, 1), (9, y_low, 0, 0)):
            there, d = beside(k)
            slot = jnp.clip(jnp.where(d > 0, d, -d) - 1, 0, 2)
            row = 0 if z else 15
            got = jnp.where(there, landing[turn][slot], zero).astype(F32)
            margin[z, :, to:to + 1, :] = got[:, row:row + 1, :]
        for dy in (-1, 0, 1):
            for dz in (-1, 0, 1):
                there, d = beside(17 * m + (dy + 1) * 3 + dz + 1)
                j = sign * d
                slot = jnp.clip(j - 1, 0, 6)
                if dy == 0 and dz == 0:
                    space[far_margin, 1:17, :, MID] = jnp.where(there, far[turn][jnp.clip(j - 1, 0, 3)], zero)
                elif dz == 0:
                    to, edge = (17, 1) if dy == 1 else (0, 2)
                    space[far_margin, to, :, MID] = jnp.where(there, far_edge[turn][slot, edge], zero)
                elif dy == 0:
                    z, edge = (1, 0) if dz == 1 else (0, 3)
                    margin[z, far_margin, 1:17, :] = jnp.where(there, far_edge[turn][slot, edge], zero).astype(F32)
                else:
                    to, edge = (17, 1) if dy == 1 else (0, 2)
                    z, row = (1, 0) if dz == 1 else (0, 15)
                    got = jnp.where(there, far_edge[turn][slot, edge], zero).astype(F32)
                    margin[z, far_margin, to:to + 1, :] = got[row:row + 1, :]

        def one(x, _):
            shift_a[8:296, :] = space[x, :, :, MID].astype(F32).reshape(288, 128)
            for z, start, row in ((0, 7, 0), (1, 9, 15)):
                shift_b[z] = shift_a[start:start + 288, :]
                shift_b.at[z][pl.ds(row, 18, stride=16), :] = margin[z, x]
                lanes = slice(256 * z, 256 * z + 128)
                space[x, :, :, lanes] = shift_b[z].reshape(18, 16, 128).astype(BF16)
            return 0

        lax.fori_loop(0, 10, one, 0)

    def conv_rows(space, weights, chunk):
        total = None
        for ex in range(3):
            for ey in range(3):
                window = space[pl.ds(2 * chunk + ex, 2), ey:ey + 16].reshape(512, 384)
                tap = ex * 9 + ey * 3
                part = dot(window, weights[tap:tap + 3].reshape(384, 128))
                total = part if total is None else total + part
        return total

    stage(pad, 0)
    copies = halo_copies(pad, 0)
    for copy in copies:
        copy.start()
    for copy in copies:
        copy.wait()
    fill(pad, 0)

    def forward(c, _):
        at = pl.ds(2 * c, 2)
        here = mask[at].reshape(512, 128)
        pre = conv_rows(pad, w_conv, c) * here
        sigmoid = 1.0 / (1.0 + jnp.exp(-pre))
        hid[...] = (pre * sigmoid).astype(BF16).astype(F32).reshape(2, 8, 2, 16, 128)
        grad = up[c].reshape(512, 128) * sigmoid * (1.0 + pre * (1.0 - sigmoid)) * here
        grad = grad.astype(BF16)
        grad_wide = grad.astype(F32)
        vol[at] = grad_wide.reshape(2, 16, 16, 128)
        gpad[pl.ds(2 * c + 1, 2), 1:17, :, MID] = grad.reshape(2, 16, 16, 128)
        for x in range(2):
            turned[2 * c + x] = grad_wide[256 * x:256 * x + 256].T.astype(BF16)
        rows = pl.ds(pl.multiple_of(64 * c, 64), 64)
        for tx in range(2):
            for ty in range(2):
                for tz in range(2):
                    t = (tx * 2 + ty) * 2 + tz
                    got = hid[tx, :, ty, pl.ds(tz, 8, stride=2), :].reshape(64, 128)
                    patches[rows, 128 * t:128 * t + 128] = got.astype(BF16)
        return 0

    lax.fori_loop(0, 4, forward, 0)

    stage(gpad, 1)
    grad_copies = halo_copies(gpad, 1)
    for copy in grad_copies:
        copy.start()

    for t in range(8):
        got = lax.dot_general(
            patches[:, 128 * t:128 * t + 128], own_cot, (((0,), (0,)), ((), ())), preferred_element_type=F32
        )
        down_st[0, 128 * t:128 * t + 128, :] = got[:, :128]
        down_st[1, 128 * t:128 * t + 128, :] = got[:, 128:]
    down_swap = remote(down_st.at[other], down_in, pair_s.at[1], pair_r.at[1], pair)
    down_swap.start()
    got = dot(patches[...], w_down[...]).astype(BF16)
    coarse_st[0] = got[:, :128]
    coarse_st[1] = got[:, 128:]
    own_half = pl.ds(pl.multiple_of(m * 256, 256), 256)
    coarse_swap = remote(coarse_st.at[other], coarse.at[own_half], pair_s.at[2], pair_r.at[2], pair)
    coarse_swap.start()
    coarse[own_half, :] = coarse_st[m]
    down_swap.wait()
    down_in[...] = down_in[...] + down_st[m]
    d_bf[...] = down_in[...].reshape(8, 128, 128).astype(BF16)
    d1 = []
    for step in range(1, ZS):
        z, device = line_peer(step)
        d1.append(remote(d_bf.at[z], d_in.at[step - 1], d1_s.at[step - 1], d1_r.at[step - 1], device))
        d1[-1].start()

    conv_swaps = []
    for ex in range(3):
        for ey in range(3):
            total = None
            for half in range(2):
                rows = pad[ex + 4 * half:ex + 4 * half + 4, ey:ey + 16].reshape(1024, 384)
                left = jnp.concatenate([turned[4 * half + x] for x in range(4)], axis=1)
                part = dot(left, rows)
                total = part if total is None else total + part
            for ez in range(3):
                tap = total[:, 128 * ez:128 * ez + 128].T
                at = ex * 9 + ey * 3 + ez
                conv_st[0, 64 * at:64 * at + 64, :] = tap[:64]
                conv_st[1, 64 * at:64 * at + 64, :] = tap[64:]
        rows = slice(576 * ex, 576 * ex + 576)
        conv_swaps.append(
            remote(conv_st.at[other, rows], conv_in.at[rows], pair_s.at[3 + ex], pair_r.at[3 + ex], pair)
        )
        conv_swaps[-1].start()
    for ex in range(3):
        rows = slice(576 * ex, 576 * ex + 576)
        conv_swaps[ex].wait()
        conv_in[rows, :] = conv_in[rows, :] + conv_st[m, rows, :]
    conv_in[1728:, :] = jnp.zeros((320, 128), F32)
    c_bf[...] = conv_in[...].reshape(16, 128, 128).astype(BF16)
    c1 = []
    for at, step in enumerate(plane_steps):
        peer, device = plane_peer(step)
        c1.append(remote(c_bf.at[peer], c_in.at[at], c1_s.at[at], c1_r.at[at], device))
        c1[-1].start()

    for copy in d1:
        copy.wait()
    d_mid[...] = down_in[pl.ds(pl.multiple_of(my_z * 128, 128), 128), :]
    for step in range(ZS - 1):
        d_mid[...] = d_mid[...] + d_in[step].astype(F32)
    d2 = []
    for at, step in enumerate(plane_steps):
        peer, device = plane_peer(step)
        rows = pl.ds(pl.multiple_of(peer * 8, 8), 8)
        d2.append(remote(d_mid.at[rows], d_in2.at[at], d2_s.at[at], d2_r.at[at], device))
        d2[-1].start()

    for copy in grad_copies:
        copy.wait()
    fill(gpad, 1)

    def backward(c, _):
        at = pl.ds(2 * c, 2)
        vol[at] = (conv_rows(gpad, w_back, c) * mask[at].reshape(512, 128)).reshape(2, 16, 16, 128)
        return 0

    lax.fori_loop(0, 2, backward, 0)

    for copy in d2:
        copy.wait()
    total = d_mid[pl.ds(pl.multiple_of(plane * 8, 8), 8), :]
    for at in range(15):
        total = total + d_in2[at]
    d_mix[plane] = total
    d3 = []
    for at, step in enumerate(plane_steps):
        peer, device = plane_peer(step)
        d3.append(remote(d_mix.at[plane], d_mix.at[plane], d3_s.at[at], d3_r.at[at], device))
        d3[-1].start()

    for copy in c1:
        copy.wait()
    own_plane = pl.ds(pl.multiple_of(plane * 128, 128), 128)
    c_mid[...] = conv_in[own_plane, :]
    for at in range(15):
        c_mid[...] = c_mid[...] + c_in[at].astype(F32)
    c2 = []
    for step in range(1, ZS):
        z, device = line_peer(step)
        rows = pl.ds(pl.multiple_of(z * 16, 16), 16)
        c2.append(remote(c_mid.at[rows], c_in2.at[step - 1], c2_s.at[step - 1], c2_r.at[step - 1], device))
        c2[-1].start()

    lax.fori_loop(2, 4, backward, 0)

    for copy in d3:
        copy.wait()
    d_tot[...] = d_mix[...].reshape(128, 128).astype(BF16)
    d_all[my_z] = d_tot[...]
    d4 = []
    for step in range(1, ZS):
        z, device = line_peer(step)
        d4.append(remote(d_tot, d_all.at[my_z], d4_s.at[step - 1], d4_r.at[step - 1], device))
        d4[-1].start()
    for copy in c2:
        copy.wait()
    own_line = pl.ds(pl.multiple_of(my_z * 16, 16), 16)
    total = c_mid[own_line, :]
    for step in range(ZS - 1):
        total = total + c_in2[step]
    c_tot[...] = total.astype(BF16)
    c_all[plane, own_line, :] = c_tot[...]
    c3 = []
    for step in range(1, ZS):
        z, device = line_peer(step)
        c3.append(remote(c_tot, c_all.at[plane, own_line], c3_s.at[step - 1], c3_r.at[step - 1], device))
        c3[-1].start()

    for oy in range(2):
        for oz in range(2):
            got = vol[:, 8 * oy:8 * oy + 8, 8 * oz:8 * oz + 8, :].reshape(512, 128)
            for part in range(2):
                columns = slice(256 * part, 256 * part + 256)
                out_bricks[oy + 2 * oz, :, columns] = got[columns].T.astype(BF16)
    feat_swap = remote(out_bricks.at[:, other_rows, :], g_feat.at[:, m], pair_s.at[6], pair_r.at[6], pair)
    feat_swap.start()
    g_feat[:, m] = out_bricks[:, own_rows, :]

    for copy in c3:
        copy.wait()
    c4 = []
    for at, step in enumerate(plane_steps):
        peer, device = plane_peer(step)
        c4.append(remote(c_all.at[plane], c_all.at[plane], c4_s.at[at], c4_r.at[at], device))
        c4[-1].start()
    for copy in d4:
        copy.wait()
    g_down[...] = d_all[...].reshape(1024, 128).astype(F32) * (1.0 / BLOCKS)
    coarse_swap.wait()
    feat_swap.wait()
    for copy in c4:
        copy.wait()
    g_conv[...] = c_all[...].reshape(2048, 128)[:1728].astype(F32) * (1.0 / BLOCKS)


def local(features, heights, neighbours, w_conv, w_down, cotangent):
    vmem = pl.BlockSpec(memory_space=pltpu.VMEM)
    smem = pl.BlockSpec(memory_space=pltpu.SMEM)
    dma = pltpu.SemaphoreType.DMA
    V = pltpu.VMEM
    scratch = [
        V((10, 18, 16, 384), BF16),
        V((10, 18, 16, 384), BF16),
        V((8, 16, 16, 128), F32),
        V((4, 2, 8, 2, 16, 128), F32),
        V((8, 16, 16, 128), F32),
        V((4, 128, 512), BF16),
        V((2, 8, 2, 16, 128), F32),
        V((256, 1024), BF16),
        V((8, 128, 256), BF16),
        V((27, 128, 128), BF16),
        V((4, 128, 512), BF16),
        V((304, 128), F32),
        V((2, 288, 128), F32),
        V((2, 10, 18, 128), F32),
        V((2, 2, 8, 16, 128), BF16),
        V((2, 4, 16, 128), BF16),
        V((3, 10, 16, 128), BF16), V((3, 10, 16, 128), BF16),
        V((3, 10, 16, 128), BF16), V((3, 10, 16, 128), BF16),
        V((2, 10, 16, 128), BF16),
        V((2, 10, 16, 128), BF16),
        V((4, 16, 16, 128), BF16), V((4, 16, 16, 128), BF16),
        V((7, 4, 16, 128), BF16), V((7, 4, 16, 128), BF16),
        V((2, 256, 128), BF16),
        V((2, 1024, 128), F32),
        V((1024, 128), F32),
        V((2, 1728, 128), F32),
        V((2048, 128), F32),
        V((16, 128, 128), BF16),
        V((15, 128, 128), BF16),
        V((128, 128), F32),
        V((7, 16, 128), F32),
        V((16, 128), BF16),
        V((16, 128, 128), BF16),
        V((8, 128, 128), BF16),
        V((7, 128, 128), BF16),
        V((128, 128), F32),
        V((15, 8, 128), F32),
        V((128, 128), BF16),
        V((16, 8, 128), F32),
        V((8, 128, 128), BF16),
        dma((2, 28)), dma((2, 28)), dma((7,)), dma((7,)),
        dma((15,)), dma((15,)), dma((7,)), dma((7,)), dma((7,)), dma((7,)), dma((15,)), dma((15,)),
        dma((7,)), dma((7,)), dma((15,)), dma((15,)), dma((15,)), dma((15,)), dma((7,)), dma((7,)),
    ]
    coarse, g_conv, g_down, g_feat = pl.pallas_call(
        kernel,
        out_shape=(
            jax.ShapeDtypeStruct((512, 128), BF16),
            jax.ShapeDtypeStruct((1728, 128), F32),
            jax.ShapeDtypeStruct((1024, 128), F32),
            jax.ShapeDtypeStruct((4, 2, 64, 512), BF16),
        ),
        in_specs=[smem, smem, vmem, vmem, vmem, vmem],
        out_specs=(vmem, vmem, vmem, vmem),
        scratch_shapes=scratch,
        compiler_params=pltpu.CompilerParams(
            collective_id=0, has_side_effects=True, vmem_limit_bytes=56 * 2**20
        ),
        cost_estimate=pl.CostEstimate(
            flops=6_000_000_000, bytes_accessed=6_000_000, transcendentals=262144
        ),
    )(
        heights,
        neighbours,
        features.transpose(0, 2, 1).reshape(4, 2, 64, 512),
        w_conv,
        w_down.reshape(1024, 256),
        cotangent[0],
    )
    return (
        coarse[None],
        g_conv.reshape(27, 64, 128),
        g_down.reshape(8, 128, 128),
        g_feat.reshape(8, 64, 512).transpose(0, 2, 1),
    )


def solution(mesh):
    placed = (
        P("space", None, "chan"),
        P("space", None),
        P("space", None),
        P(),
        P(),
        P("space", None, None),
    )
    return jax.shard_map(
        local,
        mesh=mesh,
        in_specs=placed,
        out_specs=(
            P("space", None, "chan"),
            P(None, "chan", None),
            P(None, None, "chan"),
            P("space", None, "chan"),
        ),
        check_vma=False,
    )
```

profile of v0, /device:TPU:1, one launch (start us, length us, event | category | flops | bytes accessed | tf_op | source)
XLA Modules:
  0.0 81.5 jit_solution(3799963766018297601)
XLA Ops:
  0.6 75.0 %shard_map.93 = (bf16[512,128]{1,0:T(8,128)(2,1)}, f32[1728,128]{1,0:T(8,128)}, f32[1024,128]{1,0:T(8,128)}, bf16[4,2,64,512]{3,2,1,0:T(8,128)(2,1)}) custom-call(s32[8,64]{1,0:T(8,128)} %heights.1, s32[1,26]{1,0:T(1,128)} %near.1, bf16[4,2,64,512]{3,2,1,0:T(8,128)(2,1)} %bitcast.15, bf16[27,128,128]{2,1,0:T(8,128)(2,1)} %w_conv.1, ...), custom_call_target="tpu_custom_call" | custom-call | flops 6000000000 | bytes 6000000 | tf_op jit(solution)/shard_map/pallas_call | solution.py:469
  75.7 1.6 %copy.14 = bf16[1,512,128]{2,1,0:T(8,128)(2,1)} copy(bf16[1,512,128]{2,1,0:T(8,128)(2,1)} %bitcast.14) | data formatting | bytes 262144
  77.2 0.0 copy-start.1
  77.2 2.2 %copy.15 = f32[27,64,128]{2,1,0:T(8,128)} copy(f32[27,64,128]{2,1,0:T(8,128)} %bitcast.11) | data formatting | bytes 1769472
  79.5 0.0 copy-done.1
  79.5 0.0 copy-start
  79.5 0.8 copy.16
  80.3 0.4 copy-done
  80.7 0.8 copy.17
Async XLA Ops:
  77.2 2.2 %copy-start.1 = (f32[1024,128]{1,0:T(8,128)S(1)}, f32[1024,128]{1,0:T(8,128)}, u32[]{:S(2)}) copy-start(f32[1024,128]{1,0:T(8,128)} %get-tuple-element.10) | copy-start | bytes 1572868
  79.5 1.2 %copy-start = (bf16[4,2,64,512]{3,2,1,0:T(8,128)(2,1)S(1)}, bf16[4,2,64,512]{3,2,1,0:T(8,128)(2,1)}, u32[]{:S(2)}) copy-start(bf16[4,2,64,512]{3,2,1,0:T(8,128)(2,1)} %get-tuple-element.11) | copy-start | bytes 1572868
where the time goes:
time: 83.2 us; the launch traced here: 81.5 us
  Pallas kernels  75 us (90%)
  local copies, waits for them, and re-layouts  5.83 us (7%)
    pallas_call x1, Pallas kernels, local(): pl.pallas_call(kernel, out_shape=(jax.ShapeDtypeStruct((512, 128), BF16),...  75 us
    unnamed x8, local copies, waits for them, and re-layouts  5.83 us

commit v1 on v0

v1 whole, which is shorter than its diff:
```python
import jax
import jax.numpy as jnp
from jax import lax
from jax.experimental import pallas as pl
from jax.experimental.pallas import tpu as pltpu
from jax.sharding import PartitionSpec as P

MESH = pl.DeviceIdType.MESH
F32 = jnp.float32
BF16 = jnp.bfloat16
MID = slice(128, 256)
XS, ZS, YS = 4, 8, 4
BLOCKS = XS * ZS * YS


def dot(a, b):
    return jnp.dot(a, b, preferred_element_type=F32)


def dot_t(a, b):
    return lax.dot_general(a, b, (((1,), (1,)), ((), ())), preferred_element_type=F32)


def kernel(
    heights, near, feat, w_conv_far, w_down_far, cot_far,
    coarse, c_out, d_out, g_feat,
    w_conv, w_down, cot,
    pad, gpad, mask, up, vol, cat, hid, patches, turned, w_back, out_bricks,
    shift_a, shift_b, margin,
    faces, edges, lines, y_low_0, y_low_1, y_high_0, y_high_1, z_low, z_high, far_0, far_1, far_edge_0, far_edge_1,
    line_in,
    coarse_st, down_st, down_in, conv_st, conv_in,
    c_bf, c_in, c_line, c_tot, d_bf, d_in, d_plane, d_tot,
    load, halo_s, halo_r, pair_s, pair_r,
    c1_s, c1_r, c2_s, c2_r, c3_s, c3_r, d1_s, d1_r, d2_s, d2_r, d3_s, d3_r,
):
    y_low, y_high = (y_low_0, y_low_1), (y_high_0, y_high_1)
    far, far_edge = (far_0, far_1), (far_edge_0, far_edge_1)
    s = lax.axis_index("space")
    m = lax.axis_index("chan")
    other = 1 - m
    sign = 2 * m - 1
    my_y = s % YS
    my_z = s // YS % ZS
    my_x = s // (YS * ZS)
    plane = my_x * YS + my_y
    wrap = lambda index: (index + 2 * BLOCKS) % BLOCKS
    plane_steps = [(a, b) for a in range(XS) for b in range(YS) if (a, b) != (0, 0)]

    def plane_peer(step):
        x, y = (my_x + step[0]) % XS, (my_y + step[1]) % YS
        return x * YS + y, ((x * ZS + my_z) * YS + y, m)

    def line_peer(step):
        z = (my_z + step) % ZS
        return z, ((my_x * ZS + z) * YS + my_y, m)

    def remote(src, dst, send, recv, device):
        return pltpu.make_async_remote_copy(
            src_ref=src, dst_ref=dst, send_sem=send, recv_sem=recv, device_id=device, device_id_type=MESH
        )

    barrier = pltpu.get_barrier_semaphore()
    greeted = [(s, other)]
    for d in (1, 2, 3):
        for e in (d, -d):
            greeted += [(wrap(s + e), m), (wrap(s + e), other)]
    greeted += [(wrap(s + sign * j), other) for j in (4, 5, 6, 7)]
    greeted += [plane_peer(step)[1] for step in plane_steps]
    greeted += [line_peer(step)[1] for step in range(1, ZS)]
    for device in greeted:
        pl.semaphore_signal(barrier, inc=1, device_id=device, device_id_type=MESH)

    pair = (s, other)
    own_rows = pl.ds(pl.multiple_of(m * 64, 64), 64)
    other_rows = pl.ds(pl.multiple_of(other * 64, 64), 64)
    own_half = pl.ds(pl.multiple_of(m * 256, 256), 256)
    feat_own = pltpu.make_async_copy(feat.at[:, m], cat.at[:, own_rows, :], load.at[0])
    loads = [
        pltpu.make_async_copy(w_down_far, w_down, load.at[1]),
        pltpu.make_async_copy(cot_far.at[own_half], cot, load.at[2]),
        pltpu.make_async_copy(w_conv_far, w_conv, load.at[3]),
    ]
    feat_own.start()
    for copy in loads:
        copy.start()

    pl.semaphore_wait(barrier, len(greeted))

    swap = remote(feat.at[:, other], cat.at[:, own_rows, :], pair_s.at[0], pair_r.at[0], pair)
    swap.start()
    levels = lax.broadcasted_iota(jnp.int32, (8, 128), 0)

    def mask_plane(x, _):
        for y in range(16):
            for z in range(2):
                height = heights[m + 2 * (y // 8) + 4 * z, x * 8 + y % 8]
                mask[x, y, 8 * z:8 * z + 8, :] = jnp.where(levels < height, 1.0, 0.0)
        return 0

    lax.fori_loop(0, 8, mask_plane, 0)
    feat_own.wait()
    swap.wait()

    for oy in range(2):
        for half in range(2):
            columns = slice(256 * half, 256 * half + 256)
            low = cat[oy, :, columns].astype(F32).T.reshape(4, 8, 8, 128)
            high = cat[oy + 2, :, columns].astype(F32).T.reshape(4, 8, 8, 128)
            both = jnp.concatenate([low, high], axis=2)
            at = slice(4 * half, 4 * half + 4)
            both = both * mask[at, 8 * oy:8 * oy + 8]
            vol[at, 8 * oy:8 * oy + 8] = both
            pad[1 + 4 * half:5 + 4 * half, 1 + 8 * oy:9 + 8 * oy, :, MID] = both.astype(BF16)

    near_own = 8 - 7 * m
    far_own = 1 + 7 * m
    near_margin_there = 9 * m
    near_margin = 9 - 9 * m
    far_margin = 9 * m

    def halo_copies(space, turn):
        copies = []

        def add(src, dst, device):
            at = len(copies)
            copies.append(remote(src, dst, halo_s.at[turn, at], halo_r.at[turn, at], device))

        for j in (2, 1, 3, 4):
            there = (wrap(s + sign * j), other)
            add(space.at[far_own, 1:17, :, MID], far[turn].at[j - 1], there)
        for j in (2, 1):
            for step, row, landing in ((j, 16, y_low[turn]), (-j, 1, y_high[turn])):
                at = wrap(s + step)
                add(space.at[1:9, row, :, MID], landing.at[j - 1, 1:9], (at, m))
                add(space.at[near_own, row, :, MID], landing.at[j - 1, near_margin_there], (at, other))
        for step, face, landing in ((1, 1, z_low), (-1, 0, z_high)):
            at = wrap(s + step)
            add(faces.at[turn, face], landing.at[turn, 1:9], (at, m))
            add(faces.at[turn, face, near_own - 1], landing.at[turn, near_margin_there], (at, other))
        for j in range(1, 8):
            there = (wrap(s + sign * j), other)
            which = slice(1, 3) if j <= 4 else pl.ds(2 * m, 2)
            add(edges.at[turn, which], far_edge[turn].at[j - 1, which], there)
        for step, line, side in ((3, 1, 0), (-3, 0, 1)):
            at = wrap(s + step)
            add(lines.at[turn, line], line_in.at[turn, side, 0], (at, m))
            add(lines.at[turn, line], line_in.at[turn, side, 1], (at, other))
        add(space.at[near_own, 1:17, :, MID], space.at[near_margin_there, 1:17, :, MID], pair)
        return copies

    def stage(space, turn):
        def one(x, _):
            for face, z in ((0, 0), (1, 15)):
                got = vol.at[x].reshape(256, 128)[pl.ds(z, 16, stride=16), :]
                faces[turn, face, x] = got.astype(BF16)
            return 0

        lax.fori_loop(0, 8, one, 0)
        for line, start in ((0, 0), (1, 255)):
            got = vol.reshape(2048, 128)[pl.ds(start, 8, stride=256), :]
            lines[turn, line] = jnp.concatenate([got, got], axis=0).astype(BF16)
        edges[turn, 0] = space[far_own, 1, :, MID]
        edges[turn, 1] = faces[turn, 0, far_own - 1]
        edges[turn, 2] = faces[turn, 1, far_own - 1]
        edges[turn, 3] = space[far_own, 16, :, MID]

    zero = jnp.zeros((), BF16)

    def fill(space, turn):
        def beside(k):
            got = near[0, k]
            return got >= 0, got - s

        there, d = beside(15)
        space[:, 17, :, MID] = jnp.where(there, y_high[turn][jnp.clip(d - 1, 0, 1)], zero)
        there, d = beside(10)
        space[:, 0, :, MID] = jnp.where(there, y_low[turn][jnp.clip(-d - 1, 0, 1)], zero)
        there, d = beside(13)
        margin[1, :, 1:17, :] = jnp.where(there, z_high[turn], zero).astype(F32)
        there, d = beside(12)
        margin[0, :, 1:17, :] = jnp.where(there, z_low[turn], zero).astype(F32)
        for k, landing, to, z in ((16, y_high, 17, 1), (14, y_high, 17, 0), (11, y_low, 0, 1), (9, y_low, 0, 0)):
            there, d = beside(k)
            j = jnp.where(d > 0, d, -d)
            row = 0 if z else 15
            got = jnp.where(there, landing[turn][jnp.clip(j - 1, 0, 1)], zero).astype(F32)
            got = got[:, row:row + 1, :]
            margin[z, :, to:to + 1, :] = got
            if k in (16, 9):
                side = 1 if k == 16 else 0
                third = there & (j == 3)
                line = line_in[turn, side, 0].astype(F32)[:8].reshape(8, 1, 128)
                margin[z, 1:9, to:to + 1, :] = jnp.where(third, line, got[1:9])
                beyond = line_in[turn, side, 1].astype(F32)
                beyond = jnp.where(m == 0, beyond[0:1], beyond[7:8])
                margin[z, near_margin, to:to + 1, :] = jnp.where(
                    third, beyond, jnp.where(m == 0, got[9], got[0])
                )
        for dy in (-1, 0, 1):
            for dz in (-1, 0, 1):
                there, d = beside(17 * m + (dy + 1) * 3 + dz + 1)
                j = sign * d
                slot = jnp.clip(j - 1, 0, 6)
                slot_4 = jnp.clip(j - 1, 0, 3)
                if dy == 0 and dz == 0:
                    space[far_margin, 1:17, :, MID] = jnp.where(there, far[turn][slot_4], zero)
                elif dy == 0:
                    z, edge = (1, 1) if dz == 1 else (0, 2)
                    margin[z, far_margin, 1:17, :] = jnp.where(there, far_edge[turn][slot, edge], zero).astype(F32)
                else:
                    to, edge, at = (17, 0, 0) if dy == 1 else (0, 3, 15)
                    got = jnp.where(j <= 4, far[turn][slot_4, at], far_edge[turn][slot, edge])
                    got = jnp.where(there, got, zero)
                    if dz == 0:
                        space[far_margin, to, :, MID] = got
                    else:
                        z, row = (1, 0) if dz == 1 else (0, 15)
                        margin[z, far_margin, to:to + 1, :] = got.astype(F32)[row:row + 1, :]

        def one(x, _):
            shift_a[8:296, :] = space[x, :, :, MID].astype(F32).reshape(288, 128)
            for z, start, row in ((0, 7, 0), (1, 9, 15)):
                shift_b[z] = shift_a[start:start + 288, :]
                shift_b.at[z][pl.ds(row, 18, stride=16), :] = margin[z, x]
                lanes = slice(256 * z, 256 * z + 128)
                space[x, :, :, lanes] = shift_b[z].reshape(18, 16, 128).astype(BF16)
            return 0

        lax.fori_loop(0, 10, one, 0)

    def conv_rows(space, weights, chunk):
        total = None
        for ex in range(3):
            for ey in range(3):
                window = space[pl.ds(2 * chunk + ex, 2), ey:ey + 16].reshape(512, 384)
                tap = ex * 9 + ey * 3
                part = dot(window, weights[tap:tap + 3].reshape(384, 128))
                total = part if total is None else total + part
        return total

    stage(pad, 0)
    copies = halo_copies(pad, 0)
    for copy in copies:
        copy.start()

    for copy in loads:
        copy.wait()

    def upstream(t, _):
        rows = w_down[pl.ds(pl.multiple_of(t * 256, 256), 256), :]
        got = dot_t(cot[...], rows)
        for z in range(2):
            part = got[:, 128 * z:128 * z + 128].reshape(4, 8, 8, 128)
            for x in range(4):
                up[x, t // 2, :, t % 2, pl.ds(z, 8, stride=2), :] = part[x]
        return 0

    lax.fori_loop(0, 4, upstream, 0)

    def turn_back(tap, _):
        w_back[tap] = w_conv[26 - tap].astype(F32).T.astype(BF16)
        return 0

    lax.fori_loop(0, 27, turn_back, 0)

    for copy in copies:
        copy.wait()
    fill(pad, 0)

    def forward(c, _):
        at = pl.ds(2 * c, 2)
        here = mask[at].reshape(512, 128)
        pre = conv_rows(pad, w_conv, c) * here
        sigmoid = 1.0 / (1.0 + jnp.exp(-pre))
        hid[...] = (pre * sigmoid).astype(BF16).astype(F32).reshape(2, 8, 2, 16, 128)
        grad = up[c].reshape(512, 128) * sigmoid * (1.0 + pre * (1.0 - sigmoid)) * here
        grad = grad.astype(BF16)
        grad_wide = grad.astype(F32)
        vol[at] = grad_wide.reshape(2, 16, 16, 128)
        gpad[pl.ds(2 * c + 1, 2), 1:17, :, MID] = grad.reshape(2, 16, 16, 128)
        for x in range(2):
            turned[2 * c + x] = grad_wide[256 * x:256 * x + 256].T.astype(BF16)
        rows = pl.ds(pl.multiple_of(64 * c, 64), 64)
        for tx in range(2):
            for ty in range(2):
                for tz in range(2):
                    t = (tx * 2 + ty) * 2 + tz
                    got = hid[tx, :, ty, pl.ds(tz, 8, stride=2), :].reshape(64, 128)
                    patches[rows, 128 * t:128 * t + 128] = got.astype(BF16)
        return 0

    lax.fori_loop(0, 4, forward, 0)

    for t in range(8):
        got = lax.dot_general(
            patches[:, 128 * t:128 * t + 128], cot[...], (((0,), (0,)), ((), ())), preferred_element_type=F32
        )
        down_st[0, 128 * t:128 * t + 128, :] = got[:, :128]
        down_st[1, 128 * t:128 * t + 128, :] = got[:, 128:]
    down_swap = remote(down_st.at[other], down_in, pair_s.at[1], pair_r.at[1], pair)
    down_swap.start()

    conv_swaps = []
    d1 = []
    for ex in range(3):
        for ey in range(3):
            total = None
            for half in range(2):
                rows = pad[ex + 4 * half:ex + 4 * half + 4, ey:ey + 16].reshape(1024, 384)
                left = jnp.concatenate([turned[4 * half + x] for x in range(4)], axis=1)
                part = dot(left, rows)
                total = part if total is None else total + part
            for ez in range(3):
                tap = total[:, 128 * ez:128 * ez + 128].T
                at = ex * 9 + ey * 3 + ez
                conv_st[0, 64 * at:64 * at + 64, :] = tap[:64]
                conv_st[1, 64 * at:64 * at + 64, :] = tap[64:]
        rows = slice(576 * ex, 576 * ex + 576)
        conv_swaps.append(
            remote(conv_st.at[other, rows], conv_in.at[rows], pair_s.at[3 + ex], pair_r.at[3 + ex], pair)
        )
        conv_swaps[-1].start()
        if ex == 1:
            down_swap.wait()
            down_in[...] = down_in[...] + down_st[m]
            d_bf[...] = down_in[...].reshape(8, 128, 128).astype(BF16)
            for step in range(1, ZS):
                z, device = line_peer(step)
                d1.append(remote(d_bf.at[z], d_in.at[step - 1], d1_s.at[step - 1], d1_r.at[step - 1], device))
                d1[-1].start()
    conv_in[1728:, :] = jnp.zeros((64, 128), F32)
    for ex in range(3):
        rows = slice(576 * ex, 576 * ex + 576)
        conv_swaps[ex].wait()
        conv_in[rows, :] = conv_in[rows, :] + conv_st[m, rows, :]
    c_bf[...] = conv_in[...].reshape(16, 112, 128).astype(BF16)
    c1 = []
    for at, step in enumerate(plane_steps):
        peer, device = plane_peer(step)
        c1.append(remote(c_bf.at[peer], c_in.at[at], c1_s.at[at], c1_r.at[at], device))
        c1[-1].start()

    stage(gpad, 1)
    grad_copies = halo_copies(gpad, 1)
    for copy in grad_copies:
        copy.start()
    got = dot(patches[...], w_down[...]).astype(BF16)
    coarse_st[0] = got[:, :128]
    coarse_st[1] = got[:, 128:]
    coarse_swap = remote(coarse_st.at[other], coarse.at[own_half], pair_s.at[2], pair_r.at[2], pair)
    coarse_swap.start()
    coarse_own = pltpu.make_async_copy(coarse_st.at[m], coarse.at[own_half], load.at[4])
    coarse_own.start()

    for copy in d1:
        copy.wait()
    total = down_in[pl.ds(pl.multiple_of(my_z * 128, 128), 128), :]
    for step in range(ZS - 1):
        total = total + d_in[step].astype(F32)
    d_plane[plane] = total.astype(BF16)
    d2 = []
    for at, step in enumerate(plane_steps):
        peer, device = plane_peer(step)
        d2.append(remote(d_plane.at[plane], d_plane.at[plane], d2_s.at[at], d2_r.at[at], device))
        d2[-1].start()

    for copy in c1:
        copy.wait()
    total = conv_in[pl.ds(pl.multiple_of(plane * 112, 112), 112), :]
    for at in range(15):
        total = total + c_in[at].astype(F32)
    c_line[my_z] = total.astype(BF16)
    c2 = []
    for step in range(1, ZS):
        z, device = line_peer(step)
        c2.append(remote(c_line.at[my_z], c_line.at[my_z], c2_s.at[step - 1], c2_r.at[step - 1], device))
        c2[-1].start()

    for copy in grad_copies:
        copy.wait()
    fill(gpad, 1)

    def backward(c, _):
        at = pl.ds(2 * c, 2)
        vol[at] = (conv_rows(gpad, w_back, c) * mask[at].reshape(512, 128)).reshape(2, 16, 16, 128)
        return 0

    lax.fori_loop(0, 1, backward, 0)

    for copy in c2:
        copy.wait()
    total = c_line[0].astype(F32)
    for z in range(1, ZS):
        total = total + c_line[z].astype(F32)
    c_tot[...] = total.astype(BF16)
    c3 = []
    for at, step in enumerate(plane_steps):
        peer, device = plane_peer(step)
        c3.append(remote(c_tot, c_out.at[plane], c3_s.at[at], c3_r.at[at], device))
        c3[-1].start()
    c_own = pltpu.make_async_copy(c_tot, c_out.at[plane], load.at[5])
    c_own.start()

    for copy in d2:
        copy.wait()
    total = d_plane[0].astype(F32)
    for at in range(1, 16):
        total = total + d_plane[at].astype(F32)
    d_tot[...] = total.astype(BF16)
    d3 = []
    for step in range(1, ZS):
        z, device = line_peer(step)
        d3.append(remote(d_tot, d_out.at[my_z], d3_s.at[step - 1], d3_r.at[step - 1], device))
        d3[-1].start()
    d_own = pltpu.make_async_copy(d_tot, d_out.at[my_z], load.at[6])
    d_own.start()

    lax.fori_loop(1, 4, backward, 0)

    for oy in range(2):
        for oz in range(2):
            got = vol[:, 8 * oy:8 * oy + 8, 8 * oz:8 * oz + 8, :].reshape(512, 128)
            for part in range(2):
                columns = slice(256 * part, 256 * part + 256)
                out_bricks[oy + 2 * oz, :, columns] = got[columns].T.astype(BF16)
    feat_swap = remote(out_bricks.at[:, other_rows, :], g_feat.at[:, m], pair_s.at[6], pair_r.at[6], pair)
    feat_swap.start()
    feat_out = pltpu.make_async_copy(out_bricks.at[:, own_rows, :], g_feat.at[:, m], load.at[7])
    feat_out.start()

    for copy in c3 + d3 + [coarse_swap, feat_swap, coarse_own, c_own, d_own, feat_out]:
        copy.wait()


def hand_on(c_in, d_in, coarse_in, feat_in, g_conv, g_down, coarse, g_feat, c, d, c_wide, d_wide, co, f, sems):
    held = (c, d, co, f)
    moves = [pltpu.make_async_copy(a, b, sems.at[i]) for i, (a, b) in enumerate(zip((c_in, d_in, coarse_in, feat_in), held))]
    for move in moves:
        move.start()

    def out(at, src, dst):
        move = pltpu.make_async_copy(src, dst, sems.at[at])
        move.start()
        return move

    outs = []
    moves[0].wait()
    for part in range(2):
        rows = slice(864 * part, 864 * part + 864)
        c_wide[rows, :] = c[...].reshape(1792, 128)[rows].astype(F32) * (1.0 / BLOCKS)
        outs.append(out(4 + part, c_wide.at[rows], g_conv.at[rows]))
    moves[1].wait()
    d_wide[...] = d[...].reshape(1024, 128).astype(F32) * (1.0 / BLOCKS)
    outs.append(out(6, d_wide, g_down))
    moves[2].wait()
    outs.append(out(7, co, coarse))
    moves[3].wait()
    outs.append(out(8, f, g_feat))
    for move in outs:
        move.wait()


def local(features, heights, neighbours, w_conv, w_down, cotangent):
    anywhere = pl.BlockSpec(memory_space=pl.ANY)
    smem = pl.BlockSpec(memory_space=pltpu.SMEM)
    dma = pltpu.SemaphoreType.DMA
    V = pltpu.VMEM
    scratch = [
        V((27, 128, 128), BF16), V((1024, 256), BF16), V((256, 256), BF16),
        V((10, 18, 16, 384), BF16),
        V((10, 18, 16, 384), BF16),
        V((8, 16, 16, 128), F32),
        V((4, 2, 8, 2, 16, 128), F32),
        V((8, 16, 16, 128), F32),
        V((4, 128, 512), BF16),
        V((2, 8, 2, 16, 128), F32),
        V((256, 1024), BF16),
        V((8, 128, 256), BF16),
        V((27, 128, 128), BF16),
        V((4, 128, 512), BF16),
        V((304, 128), F32),
        V((2, 288, 128), F32),
        V((2, 10, 18, 128), F32),
        V((2, 2, 8, 16, 128), BF16),
        V((2, 4, 16, 128), BF16),
        V((2, 2, 16, 128), BF16),
        V((2, 10, 16, 128), BF16), V((2, 10, 16, 128), BF16),
        V((2, 10, 16, 128), BF16), V((2, 10, 16, 128), BF16),
        V((2, 10, 16, 128), BF16),
        V((2, 10, 16, 128), BF16),
        V((4, 16, 16, 128), BF16), V((4, 16, 16, 128), BF16),
        V((7, 4, 16, 128), BF16), V((7, 4, 16, 128), BF16),
        V((2, 2, 2, 16, 128), BF16),
        V((2, 256, 128), BF16),
        V((2, 1024, 128), F32),
        V((1024, 128), F32),
        V((2, 1728, 128), F32),
        V((1792, 128), F32),
        V((16, 112, 128), BF16),
        V((15, 112, 128), BF16),
        V((8, 112, 128), BF16),
        V((112, 128), BF16),
        V((8, 128, 128), BF16),
        V((7, 128, 128), BF16),
        V((16, 128, 128), BF16),
        V((128, 128), BF16),
        dma((8,)), dma((2, 28)), dma((2, 28)), dma((7,)), dma((7,)),
        dma((15,)), dma((15,)), dma((7,)), dma((7,)), dma((15,)), dma((15,)),
        dma((7,)), dma((7,)), dma((15,)), dma((15,)), dma((7,)), dma((7,)),
    ]
    made = pl.pallas_call(
        kernel,
        out_shape=(
            jax.ShapeDtypeStruct((512, 128), BF16),
            jax.ShapeDtypeStruct((16, 112, 128), BF16),
            jax.ShapeDtypeStruct((8, 128, 128), BF16),
            jax.ShapeDtypeStruct((4, 2, 64, 512), BF16),
        ),
        in_specs=[smem, smem, anywhere, anywhere, anywhere, anywhere],
        out_specs=(anywhere,) * 4,
        scratch_shapes=scratch,
        compiler_params=pltpu.CompilerParams(
            collective_id=0, has_side_effects=True, vmem_limit_bytes=58 * 2**20
        ),
        cost_estimate=pl.CostEstimate(
            flops=6_000_000_000, bytes_accessed=6_000_000, transcendentals=262144
        ),
    )(
        heights,
        neighbours,
        features.transpose(0, 2, 1).reshape(4, 2, 64, 512),
        w_conv,
        w_down.reshape(1024, 256),
        cotangent[0],
    )
    coarse, g_conv, g_down, g_feat = made
    g_conv, g_down, coarse, g_feat = pl.pallas_call(
        hand_on,
        out_shape=(
            jax.ShapeDtypeStruct((1728, 128), F32),
            jax.ShapeDtypeStruct((1024, 128), F32),
            jax.ShapeDtypeStruct((512, 128), BF16),
            jax.ShapeDtypeStruct((4, 2, 64, 512), BF16),
        ),
        in_specs=[anywhere] * 4,
        out_specs=(anywhere,) * 4,
        scratch_shapes=[
            V((16, 112, 128), BF16), V((8, 128, 128), BF16), V((1728, 128), F32), V((1024, 128), F32),
            V((512, 128), BF16), V((4, 2, 64, 512), BF16), dma((9,)),
        ],
        compiler_params=pltpu.CompilerParams(vmem_limit_bytes=58 * 2**20),
    )(g_conv, g_down, coarse, g_feat)
    return (
        coarse[None],
        g_conv.reshape(27, 64, 128),
        g_down.reshape(8, 128, 128),
        g_feat.reshape(8, 64, 512).transpose(0, 2, 1),
    )


def solution(mesh):
    placed = (
        P("space", None, "chan"),
        P("space", None),
        P("space", None),
        P(),
        P(),
        P("space", None, None),
    )
    return jax.shard_map(
        local,
        mesh=mesh,
        in_specs=placed,
        out_specs=(
            P("space", None, "chan"),
            P(None, "chan", None),
            P(None, None, "chan"),
            P("space", None, "chan"),
        ),
        check_vma=False,
    )
```

time: 83.2 us -> 71.1 us (0.85); the launches traced: 81.5 us -> 70.9 us
  local copies, waits for them, and re-layouts: 5.83 us -> 0 us
  Pallas kernels: 75 us -> 70.3 us
    pallas_call x1, Pallas kernels: 75 us -> 67.9 us  [local(): pl.pallas_call(kernel, out_shape=(jax.ShapeDtypeStruct((512, 128), BF16),...]
    unnamed x8 -> x0, local copies, waits for them, and re-layouts: 5.83 us -> none
    pallas_call x0 -> x1, Pallas kernels: none -> 2.43 us  [local(): pl.pallas_call(hand_on, out_shape=(jax.ShapeDtypeStruct((1728, 128), F32)...]
where the time goes in v1:
time: 71.1 us; the launch traced here: 70.9 us
  Pallas kernels  70.3 us (99%)
    pallas_call x1, Pallas kernels, local(): pl.pallas_call(kernel, out_shape=(jax.ShapeDtypeStruct((512, 128), BF16),...  67.9 us
    pallas_call x1, Pallas kernels, local(): pl.pallas_call(hand_on, out_shape=(jax.ShapeDtypeStruct((1728, 128), F32)...  2.43 us

profile of v1, /device:TPU:1, one launch (start us, length us, event | category | flops | bytes accessed | tf_op | source)
XLA Modules:
  0.0 70.9 jit_solution(10649476540991374198)
XLA Ops:
  0.6 67.9 %shard_map.93 = (bf16[512,128]{1,0:T(8,128)(2,1)}, bf16[16,112,128]{2,1,0:T(8,128)(2,1)}, bf16[8,128,128]{2,1,0:T(8,128)(2,1)}, bf16[4,2,64,512]{3,2,1,0:T(8,128)(2,1)}) custom-call(s32[8,64]{1,0:T(8,128)} %heights.1, s32[1,26]{1,0:T(1,128)} %near.1, bf16[4,2,64,512]{3,2,1,0:T(8,128)(2,1)} %bitcast.12, bf16[27,128,128]{2,1,0:T(8,128)(2,1)} %w_conv_far.1, ...), custom_call_target="tpu_custom_call" | custom-call | flops 6000000000 | bytes 6000000 | tf_op jit(solution)/shard_map/pallas_call | solution.py:512
  68.5 2.4 %shard_map.94 = (f32[1728,128]{1,0:T(8,128)}, f32[1024,128]{1,0:T(8,128)}, bf16[512,128]{1,0:T(8,128)(2,1)}, bf16[4,2,64,512]{3,2,1,0:T(8,128)(2,1)}) custom-call(bf16[16,112,128]{2,1,0:T(8,128)(2,1)} %get-tuple-element.12.c_in, bf16[8,128,128]{2,1,0:T(8,128)(2,1)} %get-tuple-element.13.d_in, bf16[512,128]{1,0:T(8,128)(2,1)} %get-tuple-element.14.coarse_in, ...), custom_call_target="tpu_custom_call" | custom-call | tf_op jit(solution)/shard_map/pallas_call | solution.py:538

commit v2 on v1

--- a/solution.py
+++ b/solution.py
@@ -1,3 +1,5 @@
+import functools
+
 import jax
 import jax.numpy as jnp
 from jax import lax
@@ -22,17 +24,17 @@
 
 
 def kernel(
-    heights, near, feat, w_conv_far, w_down_far, cot_far,
+    heights_far, near_far, feat, w_conv_far, w_down_far, cot_far,
     coarse, c_out, d_out, g_feat,
-    w_conv, w_down, cot,
+    heights, near, w_conv, w_down, cot,
     pad, gpad, mask, up, vol, cat, hid, patches, turned, w_back, out_bricks,
     shift_a, shift_b, margin,
     faces, edges, lines, y_low_0, y_low_1, y_high_0, y_high_1, z_low, z_high, far_0, far_1, far_edge_0, far_edge_1,
     line_in,
     coarse_st, down_st, down_in, conv_st, conv_in,
-    c_bf, c_in, c_line, c_tot, d_bf, d_in, d_plane, d_tot,
+    c_bf, c_in, c_line, c_tot, d_bf, d_in, d_mid, d_in2, d_mix, d_tot,
     load, halo_s, halo_r, pair_s, pair_r,
-    c1_s, c1_r, c2_s, c2_r, c3_s, c3_r, d1_s, d1_r, d2_s, d2_r, d3_s, d3_r,
+    c1_s, c1_r, c2_s, c2_r, c3_s, c3_r, d1_s, d1_r, d2_s, d2_r, d3_s, d3_r, d4_s, d4_r,
 ):
     y_low, y_high = (y_low_0, y_low_1), (y_high_0, y_high_1)
     far, far_edge = (far_0, far_1), (far_edge_0, far_edge_1)
@@ -81,14 +83,19 @@
         pltpu.make_async_copy(cot_far.at[own_half], cot, load.at[2]),
         pltpu.make_async_copy(w_conv_far, w_conv, load.at[3]),
     ]
-    feat_own.start()
-    for copy in loads:
+    scalars = [
+        pltpu.make_async_copy(heights_far, heights, load.at[8]),
+        pltpu.make_async_copy(near_far, near, load.at[9]),
+    ]
+    for copy in scalars + [feat_own] + loads:
         copy.start()
 
     pl.semaphore_wait(barrier, len(greeted))
 
     swap = remote(feat.at[:, other], cat.at[:, own_rows, :], pair_s.at[0], pair_r.at[0], pair)
     swap.start()
+    for copy in scalars:
+        copy.wait()
     levels = lax.broadcasted_iota(jnp.int32, (8, 128), 0)
 
     def mask_plane(x, _):
@@ -126,9 +133,6 @@
             at = len(copies)
             copies.append(remote(src, dst, halo_s.at[turn, at], halo_r.at[turn, at], device))
 
-        for j in (2, 1, 3, 4):
-            there = (wrap(s + sign * j), other)
-            add(space.at[far_own, 1:17, :, MID], far[turn].at[j - 1], there)
         for j in (2, 1):
             for step, row, landing in ((j, 16, y_low[turn]), (-j, 1, y_high[turn])):
                 at = wrap(s + step)
@@ -138,16 +142,20 @@
             at = wrap(s + step)
             add(faces.at[turn, face], landing.at[turn, 1:9], (at, m))
             add(faces.at[turn, face, near_own - 1], landing.at[turn, near_margin_there], (at, other))
-        for j in range(1, 8):
-            there = (wrap(s + sign * j), other)
-            which = slice(1, 3) if j <= 4 else pl.ds(2 * m, 2)
-            add(edges.at[turn, which], far_edge[turn].at[j - 1, which], there)
         for step, line, side in ((3, 1, 0), (-3, 0, 1)):
             at = wrap(s + step)
             add(lines.at[turn, line], line_in.at[turn, side, 0], (at, m))
             add(lines.at[turn, line], line_in.at[turn, side, 1], (at, other))
         add(space.at[near_own, 1:17, :, MID], space.at[near_margin_there, 1:17, :, MID], pair)
-        return copies
+        beside = len(copies)
+        for j in range(1, 8):
+            there = (wrap(s + sign * j), other)
+            which = slice(1, 3) if j <= 4 else pl.ds(2 * m, 2)
+            add(edges.at[turn, which], far_edge[turn].at[j - 1, which], there)
+        for j in (2, 1, 3, 4):
+            there = (wrap(s + sign * j), other)
+            add(space.at[far_own, 1:17, :, MID], far[turn].at[j - 1], there)
+        return copies[:beside], copies[beside:]
 
     def stage(space, turn):
         def one(x, _):
@@ -167,11 +175,20 @@
 
     zero = jnp.zeros((), BF16)
 
-    def fill(space, turn):
-        def beside(k):
-            got = near[0, k]
-            return got >= 0, got - s
-
+    def beside(k):
+        got = near[0, k]
+        return got >= 0, got - s
+
+    def shift(space, x, _):
+        shift_a[8:296, :] = space[x, :, :, MID].astype(F32).reshape(288, 128)
+        for z, start, row in ((0, 7, 0), (1, 9, 15)):
+            shift_b[z] = shift_a[start:start + 288, :]
+            shift_b.at[z][pl.ds(row, 18, stride=16), :] = margin[z, x]
+            lanes = slice(256 * z, 256 * z + 128)
+            space[x, :, :, lanes] = shift_b[z].reshape(18, 16, 128).astype(BF16)
+        return 0
+
+    def fill_beside(space, turn):
         there, d = beside(15)
         space[:, 17, :, MID] = jnp.where(there, y_high[turn][jnp.clip(d - 1, 0, 1)], zero)
         there, d = beside(10)
@@ -197,6 +214,9 @@
                 margin[z, near_margin, to:to + 1, :] = jnp.where(
                     third, beyond, jnp.where(m == 0, got[9], got[0])
                 )
+        lax.fori_loop(1 - m, 10 - m, functools.partial(shift, space), 0)
+
+    def fill_far(space, turn):
         for dy in (-1, 0, 1):
             for dz in (-1, 0, 1):
                 there, d = beside(17 * m + (dy + 1) * 3 + dz + 1)
@@ -218,16 +238,7 @@
                         z, row = (1, 0) if dz == 1 else (0, 15)
                         margin[z, far_margin, to:to + 1, :] = got.astype(F32)[row:row + 1, :]
 
-        def one(x, _):
-            shift_a[8:296, :] = space[x, :, :, MID].astype(F32).reshape(288, 128)
-            for z, start, row in ((0, 7, 0), (1, 9, 15)):
-                shift_b[z] = shift_a[start:start + 288, :]
-                shift_b.at[z][pl.ds(row, 18, stride=16), :] = margin[z, x]
-                lanes = slice(256 * z, 256 * z + 128)
-                space[x, :, :, lanes] = shift_b[z].reshape(18, 16, 128).astype(BF16)
-            return 0
-
-        lax.fori_loop(0, 10, one, 0)
+        shift(space, far_margin, 0)
 
     def conv_rows(space, weights, chunk):
         total = None
@@ -240,8 +251,8 @@
         return total
 
     stage(pad, 0)
-    copies = halo_copies(pad, 0)
-    for copy in copies:
+    copies_beside, copies_far = halo_copies(pad, 0)
+    for copy in copies_beside + copies_far:
         copy.start()
 
     for copy in loads:
@@ -264,11 +275,12 @@
 
     lax.fori_loop(0, 27, turn_back, 0)
 
-    for copy in copies:
-        copy.wait()
-    fill(pad, 0)
-
-    def forward(c, _):
+    for copy in copies_beside:
+        copy.wait()
+    fill_beside(pad, 0)
+
+    def forward(step, _):
+        c = jnp.where(m == 0, 3 - step, step)
         at = pl.ds(2 * c, 2)
         here = mask[at].reshape(512, 128)
         pre = conv_rows(pad, w_conv, c) * here
@@ -290,7 +302,17 @@
                     patches[rows, 128 * t:128 * t + 128] = got.astype(BF16)
         return 0
 
-    lax.fori_loop(0, 4, forward, 0)
+    lax.fori_loop(0, 3, forward, 0)
+    for copy in copies_far:
+        copy.wait()
+    fill_far(pad, 0)
+    lax.fori_loop(3, 4, forward, 0)
+
+    stage(gpad, 1)
+    grad_beside, grad_far = halo_copies(gpad, 1)
+    grad_copies = grad_beside + grad_far
+    for copy in grad_copies:
+        copy.start()
 
     for t in range(8):
         got = lax.dot_general(
@@ -341,10 +363,6 @@
         c1.append(remote(c_bf.at[peer], c_in.at[at], c1_s.at[at], c1_r.at[at], device))
         c1[-1].start()
 
-    stage(gpad, 1)
-    grad_copies = halo_copies(gpad, 1)
-    for copy in grad_copies:
-        copy.start()
     got = dot(patches[...], w_down[...]).astype(BF16)
     coarse_st[0] = got[:, :128]
     coarse_st[1] = got[:, 128:]
@@ -358,13 +376,13 @@
     total = down_in[pl.ds(pl.multiple_of(my_z * 128, 128), 128), :]
     for step in range(ZS - 1):
         total = total + d_in[step].astype(F32)
-    d_plane[plane] = total.astype(BF16)
+    d_mid[...] = total
     d2 = []
     for at, step in enumerate(plane_steps):
         peer, device = plane_peer(step)
-        d2.append(remote(d_plane.at[plane], d_plane.at[plane], d2_s.at[at], d2_r.at[at], device))
+        rows = pl.ds(pl.multiple_of(peer * 8, 8), 8)
+        d2.append(remote(d_mid.at[rows], d_in2.at[at], d2_s.at[at], d2_r.at[at], device))
         d2[-1].start()
-
     for copy in c1:
         copy.wait()
     total = conv_in[pl.ds(pl.multiple_of(plane * 112, 112), 112), :]
@@ -377,17 +395,17 @@
         c2.append(remote(c_line.at[my_z], c_line.at[my_z], c2_s.at[step - 1], c2_r.at[step - 1], device))
         c2[-1].start()
 
-    for copy in grad_copies:
-        copy.wait()
-    fill(gpad, 1)
-
-    def backward(c, _):
-        at = pl.ds(2 * c, 2)
-        vol[at] = (conv_rows(gpad, w_back, c) * mask[at].reshape(512, 128)).reshape(2, 16, 16, 128)
-        return 0
-
-    lax.fori_loop(0, 1, backward, 0)
-
+    for copy in d2:
+        copy.wait()
+    total = d_mid[pl.ds(pl.multiple_of(plane * 8, 8), 8), :]
+    for at in range(15):
+        total = total + d_in2[at]
+    d_mix[plane] = total
+    d4 = []
+    for at, step in enumerate(plane_steps):
+        peer, device = plane_peer(step)
+        d4.append(remote(d_mix.at[plane], d_mix.at[plane], d4_s.at[at], d4_r.at[at], device))
+        d4[-1].start()
     for copy in c2:
         copy.wait()
     total = c_line[0].astype(F32)
@@ -402,12 +420,9 @@
     c_own = pltpu.make_async_copy(c_tot, c_out.at[plane], load.at[5])
     c_own.start()
 
-    for copy in d2:
-        copy.wait()
-    total = d_plane[0].astype(F32)
-    for at in range(1, 16):
-        total = total + d_plane[at].astype(F32)
-    d_tot[...] = total.astype(BF16)
+    for copy in d4:
+        copy.wait()
+    d_tot[...] = d_mix[...].reshape(128, 128).astype(BF16)
     d3 = []
     for step in range(1, ZS):
         z, device = line_peer(step)
@@ -416,7 +431,17 @@
     d_own = pltpu.make_async_copy(d_tot, d_out.at[my_z], load.at[6])
     d_own.start()
 
-    lax.fori_loop(1, 4, backward, 0)
+    for copy in grad_copies:
+        copy.wait()
+    fill_beside(gpad, 1)
+    fill_far(gpad, 1)
+
+    def backward(c, _):
+        at = pl.ds(2 * c, 2)
+        vol[at] = (conv_rows(gpad, w_back, c) * mask[at].reshape(512, 128)).reshape(2, 16, 16, 128)
+        return 0
+
+    lax.fori_loop(0, 4, backward, 0)
 
     for oy in range(2):
         for oz in range(2):
@@ -463,10 +488,10 @@
 
 def local(features, heights, neighbours, w_conv, w_down, cotangent):
     anywhere = pl.BlockSpec(memory_space=pl.ANY)
-    smem = pl.BlockSpec(memory_space=pltpu.SMEM)
     dma = pltpu.SemaphoreType.DMA
     V = pltpu.VMEM
     scratch = [
+        pltpu.SMEM((8, 64), jnp.int32), pltpu.SMEM((1, 26), jnp.int32),
         V((27, 128, 128), BF16), V((1024, 256), BF16), V((256, 256), BF16),
         V((10, 18, 16, 384), BF16),
         V((10, 18, 16, 384), BF16),
@@ -503,11 +528,11 @@
         V((112, 128), BF16),
         V((8, 128, 128), BF16),
         V((7, 128, 128), BF16),
-        V((16, 128, 128), BF16),
+        V((128, 128), F32), V((15, 8, 128), F32), V((16, 8, 128), F32),
         V((128, 128), BF16),
-        dma((8,)), dma((2, 28)), dma((2, 28)), dma((7,)), dma((7,)),
+        dma((10,)), dma((2, 28)), dma((2, 28)), dma((7,)), dma((7,)),
         dma((15,)), dma((15,)), dma((7,)), dma((7,)), dma((15,)), dma((15,)),
-        dma((7,)), dma((7,)), dma((15,)), dma((15,)), dma((7,)), dma((7,)),
+        dma((7,)), dma((7,)), dma((15,)), dma((15,)), dma((7,)), dma((7,)), dma((15,)), dma((15,)),
     ]
     made = pl.pallas_call(
         kernel,
@@ -517,7 +542,7 @@
             jax.ShapeDtypeStruct((8, 128, 128), BF16),
             jax.ShapeDtypeStruct((4, 2, 64, 512), BF16),
         ),
-        in_specs=[smem, smem, anywhere, anywhere, anywhere, anywhere],
+        in_specs=[anywhere] * 6,
         out_specs=(anywhere,) * 4,
         scratch_shapes=scratch,
         compiler_params=pltpu.CompilerParams(

time: 71.1 us -> 63.8 us (0.90)
  Pallas kernels: 70.3 us -> 63.1 us
    pallas_call x1, Pallas kernels: 67.9 us -> 60.7 us  [local(): pl.pallas_call(kernel, out_shape=(jax.ShapeDtypeStruct((512, 128), BF16),...]
where the time goes in v2:
time: 63.8 us; the launch traced here: 63.7 us
  Pallas kernels  63.1 us (99%)
  between operations  0.64 us (1%)
    pallas_call x1, Pallas kernels, local(): pl.pallas_call(kernel, out_shape=(jax.ShapeDtypeStruct((512, 128), BF16),...  60.7 us
    pallas_call x1, Pallas kernels, local(): pl.pallas_call(hand_on, out_shape=(jax.ShapeDtypeStruct((1728, 128), F32)...  2.43 us

profile of v2, /device:TPU:1, one launch (start us, length us, event | category | flops | bytes accessed | tf_op | source)
XLA Modules:
  0.0 63.7 jit_solution(4623377026755491410)
XLA Ops:
  0.6 60.7 %shard_map.93 = (bf16[512,128]{1,0:T(8,128)(2,1)}, bf16[16,112,128]{2,1,0:T(8,128)(2,1)}, bf16[8,128,128]{2,1,0:T(8,128)(2,1)}, bf16[4,2,64,512]{3,2,1,0:T(8,128)(2,1)}) custom-call(s32[8,64]{1,0:T(8,128)} %heights_far.1, s32[1,26]{1,0:T(1,128)} %near_far.1, bf16[4,2,64,512]{3,2,1,0:T(8,128)(2,1)} %bitcast.12, bf16[27,128,128]{2,1,0:T(8,128)(2,1)} %w_conv_far.1, ...), custom_call_target="tpu_custom_call" | custom-call | flops 6000000000 | bytes 6000000 | tf_op jit(solution)/shard_map/pallas_call | solution.py:537
  61.3 2.4 %shard_map.94 = (f32[1728,128]{1,0:T(8,128)}, f32[1024,128]{1,0:T(8,128)}, bf16[512,128]{1,0:T(8,128)(2,1)}, bf16[4,2,64,512]{3,2,1,0:T(8,128)(2,1)}) custom-call(bf16[16,112,128]{2,1,0:T(8,128)(2,1)} %get-tuple-element.12.c_in, bf16[8,128,128]{2,1,0:T(8,128)(2,1)} %get-tuple-element.13.d_in, bf16[512,128]{1,0:T(8,128)(2,1)} %get-tuple-element.14.coarse_in, ...), custom_call_target="tpu_custom_call" | custom-call | tf_op jit(solution)/shard_map/pallas_call | solution.py:563

commit v3 on v2

--- a/solution.py
+++ b/solution.py
@@ -47,7 +47,10 @@
     my_x = s // (YS * ZS)
     plane = my_x * YS + my_y
     wrap = lambda index: (index + 2 * BLOCKS) % BLOCKS
+    hops = lambda step, size: min(step, size - step)
     plane_steps = [(a, b) for a in range(XS) for b in range(YS) if (a, b) != (0, 0)]
+    plane_steps.sort(key=lambda step: -hops(step[0], XS) - hops(step[1], YS))
+    line_steps = sorted(range(1, ZS), key=lambda step: -hops(step, ZS))
 
     def plane_peer(step):
         x, y = (my_x + step[0]) % XS, (my_y + step[1]) % YS
@@ -69,7 +72,7 @@
             greeted += [(wrap(s + e), m), (wrap(s + e), other)]
     greeted += [(wrap(s + sign * j), other) for j in (4, 5, 6, 7)]
     greeted += [plane_peer(step)[1] for step in plane_steps]
-    greeted += [line_peer(step)[1] for step in range(1, ZS)]
+    greeted += [line_peer(step)[1] for step in line_steps]
     for device in greeted:
         pl.semaphore_signal(barrier, inc=1, device_id=device, device_id_type=MESH)
 
@@ -285,7 +288,7 @@
         here = mask[at].reshape(512, 128)
         pre = conv_rows(pad, w_conv, c) * here
         sigmoid = 1.0 / (1.0 + jnp.exp(-pre))
-        hid[...] = (pre * sigmoid).astype(BF16).astype(F32).reshape(2, 8, 2, 16, 128)
+        hid[c] = (pre * sigmoid).astype(BF16).astype(F32).reshape(2, 8, 2, 16, 128)
         grad = up[c].reshape(512, 128) * sigmoid * (1.0 + pre * (1.0 - sigmoid)) * here
         grad = grad.astype(BF16)
         grad_wide = grad.astype(F32)
@@ -298,11 +301,12 @@
             for ty in range(2):
                 for tz in range(2):
                     t = (tx * 2 + ty) * 2 + tz
-                    got = hid[tx, :, ty, pl.ds(tz, 8, stride=2), :].reshape(64, 128)
+                    got = hid[c, tx, :, ty, pl.ds(tz, 8, stride=2), :].reshape(64, 128)
                     patches[rows, 128 * t:128 * t + 128] = got.astype(BF16)
         return 0
 
-    lax.fori_loop(0, 3, forward, 0)
+    for step in range(3):
+        forward(step, 0)
     for copy in copies_far:
         copy.wait()
     fill_far(pad, 0)
@@ -311,7 +315,7 @@
     stage(gpad, 1)
     grad_beside, grad_far = halo_copies(gpad, 1)
     grad_copies = grad_beside + grad_far
-    for copy in grad_copies:
+    for copy in grad_beside:
         copy.start()
 
     for t in range(8):
@@ -326,18 +330,19 @@
     conv_swaps = []
     d1 = []
     for ex in range(3):
-        for ey in range(3):
-            total = None
-            for half in range(2):
-                rows = pad[ex + 4 * half:ex + 4 * half + 4, ey:ey + 16].reshape(1024, 384)
-                left = jnp.concatenate([turned[4 * half + x] for x in range(4)], axis=1)
-                part = dot(left, rows)
-                total = part if total is None else total + part
-            for ez in range(3):
-                tap = total[:, 128 * ez:128 * ez + 128].T
-                at = ex * 9 + ey * 3 + ez
-                conv_st[0, 64 * at:64 * at + 64, :] = tap[:64]
-                conv_st[1, 64 * at:64 * at + 64, :] = tap[64:]
+        total = None
+        for part in range(4):
+            rows = jnp.concatenate(
+                [pad[ex + 2 * part:ex + 2 * part + 2, ey:ey + 16].reshape(512, 384) for ey in range(3)], axis=1
+            )
+            left = jnp.concatenate([turned[2 * part + x] for x in range(2)], axis=1)
+            got = dot(left, rows)
+            total = got if total is None else total + got
+        for tap in range(9):
+            turn = total[:, 128 * tap:128 * tap + 128].T
+            at = ex * 9 + tap
+            conv_st[0, 64 * at:64 * at + 64, :] = turn[:64]
+            conv_st[1, 64 * at:64 * at + 64, :] = turn[64:]
         rows = slice(576 * ex, 576 * ex + 576)
         conv_swaps.append(
             remote(conv_st.at[other, rows], conv_in.at[rows], pair_s.at[3 + ex], pair_r.at[3 + ex], pair)
@@ -347,7 +352,7 @@
             down_swap.wait()
             down_in[...] = down_in[...] + down_st[m]
             d_bf[...] = down_in[...].reshape(8, 128, 128).astype(BF16)
-            for step in range(1, ZS):
+            for step in line_steps:
                 z, device = line_peer(step)
                 d1.append(remote(d_bf.at[z], d_in.at[step - 1], d1_s.at[step - 1], d1_r.at[step - 1], device))
                 d1[-1].start()
@@ -390,10 +395,12 @@
         total = total + c_in[at].astype(F32)
     c_line[my_z] = total.astype(BF16)
     c2 = []
-    for step in range(1, ZS):
+    for step in line_steps:
         z, device = line_peer(step)
         c2.append(remote(c_line.at[my_z], c_line.at[my_z], c2_s.at[step - 1], c2_r.at[step - 1], device))
         c2[-1].start()
+    for copy in grad_far:
+        copy.start()
 
     for copy in d2:
         copy.wait()
@@ -424,24 +431,28 @@
         copy.wait()
     d_tot[...] = d_mix[...].reshape(128, 128).astype(BF16)
     d3 = []
-    for step in range(1, ZS):
+    for step in line_steps:
         z, device = line_peer(step)
         d3.append(remote(d_tot, d_out.at[my_z], d3_s.at[step - 1], d3_r.at[step - 1], device))
         d3[-1].start()
     d_own = pltpu.make_async_copy(d_tot, d_out.at[my_z], load.at[6])
     d_own.start()
 
-    for copy in grad_copies:
+    for copy in grad_beside:
         copy.wait()
     fill_beside(gpad, 1)
-    fill_far(gpad, 1)
-
-    def backward(c, _):
+
+    def backward(step, _):
+        c = jnp.where(m == 0, 3 - step, step)
         at = pl.ds(2 * c, 2)
         vol[at] = (conv_rows(gpad, w_back, c) * mask[at].reshape(512, 128)).reshape(2, 16, 16, 128)
         return 0
 
-    lax.fori_loop(0, 4, backward, 0)
+    lax.fori_loop(0, 3, backward, 0)
+    for copy in grad_far:
+        copy.wait()
+    fill_far(gpad, 1)
+    backward(3, 0)
 
     for oy in range(2):
         for oz in range(2):
@@ -499,7 +510,7 @@
         V((4, 2, 8, 2, 16, 128), F32),
         V((8, 16, 16, 128), F32),
         V((4, 128, 512), BF16),
-        V((2, 8, 2, 16, 128), F32),
+        V((4, 2, 8, 2, 16, 128), F32),
         V((256, 1024), BF16),
         V((8, 128, 256), BF16),
         V((27, 128, 128), BF16),

time: 63.8 us -> 61.7 us (0.967)
  Pallas kernels: 63.1 us -> 60.9 us
    pallas_call x1, Pallas kernels: 60.7 us -> 58.5 us  [local(): pl.pallas_call(kernel, out_shape=(jax.ShapeDtypeStruct((512, 128), BF16),...]
where the time goes in v3:
time: 61.7 us; the launch traced here: 61.6 us
  Pallas kernels  60.9 us (99%)
  between operations  0.64 us (1%)
    pallas_call x1, Pallas kernels, local(): pl.pallas_call(kernel, out_shape=(jax.ShapeDtypeStruct((512, 128), BF16),...  58.5 us
    pallas_call x1, Pallas kernels, local(): pl.pallas_call(hand_on, out_shape=(jax.ShapeDtypeStruct((1728, 128), F32)...  2.43 us

profile of v3, /device:TPU:1, one launch (start us, length us, event | category | flops | bytes accessed | tf_op | source)
XLA Modules:
  0.0 61.6 jit_solution(11431460380860431139)
XLA Ops:
  0.6 58.5 %shard_map.93 = (bf16[512,128]{1,0:T(8,128)(2,1)}, bf16[16,112,128]{2,1,0:T(8,128)(2,1)}, bf16[8,128,128]{2,1,0:T(8,128)(2,1)}, bf16[4,2,64,512]{3,2,1,0:T(8,128)(2,1)}) custom-call(s32[8,64]{1,0:T(8,128)} %heights_far.1, s32[1,26]{1,0:T(1,128)} %near_far.1, bf16[4,2,64,512]{3,2,1,0:T(8,128)(2,1)} %bitcast.12, bf16[27,128,128]{2,1,0:T(8,128)(2,1)} %w_conv_far.1, ...), custom_call_target="tpu_custom_call" | custom-call | flops 6000000000 | bytes 6000000 | tf_op jit(solution)/shard_map/pallas_call | solution.py:548
  59.1 2.4 %shard_map.94 = (f32[1728,128]{1,0:T(8,128)}, f32[1024,128]{1,0:T(8,128)}, bf16[512,128]{1,0:T(8,128)(2,1)}, bf16[4,2,64,512]{3,2,1,0:T(8,128)(2,1)}) custom-call(bf16[16,112,128]{2,1,0:T(8,128)(2,1)} %get-tuple-element.12.c_in, bf16[8,128,128]{2,1,0:T(8,128)(2,1)} %get-tuple-element.13.d_in, bf16[512,128]{1,0:T(8,128)(2,1)} %get-tuple-element.14.coarse_in, ...), custom_call_target="tpu_custom_call" | custom-call | tf_op jit(solution)/shard_map/pallas_call | solution.py:574

commit v4 on v3

--- a/solution.py
+++ b/solution.py
@@ -376,18 +376,6 @@
     coarse_own = pltpu.make_async_copy(coarse_st.at[m], coarse.at[own_half], load.at[4])
     coarse_own.start()
 
-    for copy in d1:
-        copy.wait()
-    total = down_in[pl.ds(pl.multiple_of(my_z * 128, 128), 128), :]
-    for step in range(ZS - 1):
-        total = total + d_in[step].astype(F32)
-    d_mid[...] = total
-    d2 = []
-    for at, step in enumerate(plane_steps):
-        peer, device = plane_peer(step)
-        rows = pl.ds(pl.multiple_of(peer * 8, 8), 8)
-        d2.append(remote(d_mid.at[rows], d_in2.at[at], d2_s.at[at], d2_r.at[at], device))
-        d2[-1].start()
     for copy in c1:
         copy.wait()
     total = conv_in[pl.ds(pl.multiple_of(plane * 112, 112), 112), :]
@@ -402,6 +390,18 @@
     for copy in grad_far:
         copy.start()
 
+    for copy in d1:
+        copy.wait()
+    total = down_in[pl.ds(pl.multiple_of(my_z * 128, 128), 128), :]
+    for step in range(ZS - 1):
+        total = total + d_in[step].astype(F32)
+    d_mid[...] = total
+    d2 = []
+    for at, step in enumerate(plane_steps):
+        peer, device = plane_peer(step)
+        rows = pl.ds(pl.multiple_of(peer * 8, 8), 8)
+        d2.append(remote(d_mid.at[rows], d_in2.at[at], d2_s.at[at], d2_r.at[at], device))
+        d2[-1].start()
     for copy in d2:
         copy.wait()
     total = d_mid[pl.ds(pl.multiple_of(plane * 8, 8), 8), :]

time: 61.7 us -> 66.1 us (1.071)
  Pallas kernels: 60.9 us -> 65.4 us
    pallas_call x1, Pallas kernels: 58.5 us -> 62.9 us  [local(): pl.pallas_call(kernel, out_shape=(jax.ShapeDtypeStruct((512, 128), BF16),...]
where the time goes in v4:
time: 66.1 us; the launch traced here: 66 us
  Pallas kernels  65.4 us (99%)
    pallas_call x1, Pallas kernels, local(): pl.pallas_call(kernel, out_shape=(jax.ShapeDtypeStruct((512, 128), BF16),...  62.9 us
    pallas_call x1, Pallas kernels, local(): pl.pallas_call(hand_on, out_shape=(jax.ShapeDtypeStruct((1728, 128), F32)...  2.43 us

profile of v4, /device:TPU:1, one launch (start us, length us, event | category | flops | bytes accessed | tf_op | source)
XLA Modules:
  0.0 66.0 jit_solution(10633538530127481395)
XLA Ops:
  0.6 62.9 %shard_map.93 = (bf16[512,128]{1,0:T(8,128)(2,1)}, bf16[16,112,128]{2,1,0:T(8,128)(2,1)}, bf16[8,128,128]{2,1,0:T(8,128)(2,1)}, bf16[4,2,64,512]{3,2,1,0:T(8,128)(2,1)}) custom-call(s32[8,64]{1,0:T(8,128)} %heights_far.1, s32[1,26]{1,0:T(1,128)} %near_far.1, bf16[4,2,64,512]{3,2,1,0:T(8,128)(2,1)} %bitcast.12, bf16[27,128,128]{2,1,0:T(8,128)(2,1)} %w_conv_far.1, ...), custom_call_target="tpu_custom_call" | custom-call | flops 6000000000 | bytes 6000000 | tf_op jit(solution)/shard_map/pallas_call | solution.py:548
  63.6 2.4 %shard_map.94 = (f32[1728,128]{1,0:T(8,128)}, f32[1024,128]{1,0:T(8,128)}, bf16[512,128]{1,0:T(8,128)(2,1)}, bf16[4,2,64,512]{3,2,1,0:T(8,128)(2,1)}) custom-call(bf16[16,112,128]{2,1,0:T(8,128)(2,1)} %get-tuple-element.12.c_in, bf16[8,128,128]{2,1,0:T(8,128)(2,1)} %get-tuple-element.13.d_in, bf16[512,128]{1,0:T(8,128)(2,1)} %get-tuple-element.14.coarse_in, ...), custom_call_target="tpu_custom_call" | custom-call | tf_op jit(solution)/shard_map/pallas_call | solution.py:574
